TPU v7x, 32 devices: a whole 2x2x4 slice. The times are simulated.
32 devices in a mesh: groups: 2 (over y), ctx: 4 (over z), tp: 4 (over x, core).
Axes of the slice: x: 2, y: 2, z: 4, core: 2. Of those that a mesh axis runs over, the one named last changes fastest.
Arguments:
- queries: bfloat16 [2048, 64, 128], P(('groups', 'ctx'), 'tp'), parts along dimension 0, may hold values from -4.5 to 4.5
- keys: bfloat16 [2048, 8, 128], P(('groups', 'ctx'), 'tp'), parts along dimension 0, may hold values from -5.5 to 5.5
- values: bfloat16 [2048, 8, 128], P(('groups', 'ctx'), 'tp'), parts along dimension 0, may hold values from -6 to 6
- doc_pos: int32 [2048], P(('groups', 'ctx')), parts along dimension 0, may hold values from 0 to 511, as said below
- log_decay: float32 [2048, 64], P(('groups', 'ctx'), 'tp'), parts along dimension 0, may hold values from -0.8 to 0
- student_c: bfloat16 [2048, 64, 128], P(('groups', 'ctx'), 'tp'), parts along dimension 0, may hold values from -6 to 6
- student_write: bfloat16 [2048, 8, 128], P(('groups', 'ctx'), 'tp'), parts along dimension 0, may hold values from -6 to 6
- student_input: bfloat16 [2048, 8, 128], P(('groups', 'ctx'), 'tp'), parts along dimension 0, may hold values from -46 to 46
- gain: float32 [64, 128], P('tp'), may hold values from 0.5 to 1.5
Outputs:
- readout_gradient: bfloat16 [2048, 64, 128], P(('groups', 'ctx'), 'tp'), parts along dimension 0
- write_gradient: bfloat16 [2048, 8, 128], P(('groups', 'ctx'), 'tp'), parts along dimension 0
- input_gradient: bfloat16 [2048, 8, 128], P(('groups', 'ctx'), 'tp'), parts along dimension 0
- grad_gain: float32 [128, 128], P(('groups', 'tp')), parts along dimension 0
There are 2 independent parts, one for each index of `groups`. A program takes and returns all parts, laid end to end along the dimension named above; an argument that names none is the same for every part. Nothing has to cross between parts.
Inputs may be any that keep to these rules, and one draw needn't show every extreme that they name: `doc_pos`: every document starts with position 0 and counts up by one a token; the first token starts a document; the longest document has exactly 512 tokens.
All inputs are finite; a program needn't handle non-finite values.
Results may differ from a plain program's by a relative error of at most 0.0075.
Values may be sent and summed in bfloat16 or wider, within the bound.
A program may use at most 128 MiB of HBM per device.

v0:
```python
import math
import jax
import jax.numpy as jnp
from jax import lax
from jax.sharding import PartitionSpec as P

EPSILON = 1e-05
STUDENT_FLOOR = 1.0
NEG_FLOOR = -1e30


def entering(value, axis, join, neutral, backward):
    count, mine = (lax.axis_size(axis), lax.axis_index(axis))
    pieces = jax.tree.map(lambda part: lax.all_gather(part, axis), value)
    if backward:
        pieces = jax.tree.map(lambda part: part[::-1], pieces)
        mine = count - 1 - mine
    so_far = jax.tree.map(
        lambda part, zero: jnp.full_like(part, 0) + jnp.asarray(zero, part.dtype), value, neutral
    )

    def step(position, so_far):
        longer = join(so_far, jax.tree.map(lambda part: part[position], pieces))
        return jax.tree.map(lambda new, old: jnp.where(position < mine, new, old), longer, so_far)

    return lax.fori_loop(0, count - 1, step, so_far)


def chain_states(earlier, later):
    decay_one, state_one = earlier
    decay_two, state_two = later
    return (decay_one * decay_two, decay_two[:, None, None] * state_one + state_two)


def attend_block(running, key_tile, value_block, key_first, queries, positions, doc_start):
    best, accum = running
    tok_rows, head_count, head_width = queries.shape
    group_count = key_tile.shape[1]
    repeat = head_count // group_count
    block_rows = key_tile.shape[0]
    key_positions = key_first + jnp.arange(block_rows, dtype=jnp.int32)
    visible = (key_positions[None, :] <= positions[:, None]) & (
        key_positions[None, :] >= doc_start[:, None]
    )
    grouped_rows = queries.reshape(tok_rows, group_count, repeat, head_width)
    score_matrix = jnp.einsum(
        "yubk,ouk->ubyo", grouped_rows, key_tile, preferred_element_type=jnp.float32
    )
    score_matrix = score_matrix.reshape(head_count, tok_rows, block_rows) * (
        1.0 / math.sqrt(head_width)
    )
    score_matrix = jnp.where(visible[None], score_matrix, -jnp.inf)
    new_best = jnp.maximum(best, jnp.max(score_matrix, axis=-1))
    weights = jnp.exp(score_matrix - new_best[..., None]).astype(jnp.bfloat16)
    mixed_out = jnp.einsum(
        "hvbc,chw->hvbw",
        weights.reshape(group_count, repeat, tok_rows, block_rows),
        value_block,
        preferred_element_type=jnp.float32,
    )
    accum = accum * jnp.exp(best - new_best)[..., None] + mixed_out.reshape(
        head_count, tok_rows, head_width
    )
    return (new_best, accum)


def fold_keys(running, pieces, queries, positions, doc_start):
    key_rows, value_rows = pieces
    count = key_rows.shape[0]
    block_rows = math.gcd(count, 512)
    lowest = jnp.min(doc_start)
    highest = positions[-1]

    def one_step(current, block_index):
        key_first = block_index * block_rows
        key_tile = lax.dynamic_slice_in_dim(key_rows, block_index * block_rows, block_rows, 0)
        value_block = lax.dynamic_slice_in_dim(value_rows, block_index * block_rows, block_rows, 0)
        needed = (key_first <= highest) & (key_first + block_rows - 1 >= lowest)

        def update(inside):
            return attend_block(
                inside, key_tile, value_block, key_first, queries, positions, doc_start
            )

        def unchanged(inside):
            return inside

        return (lax.cond(needed, update, unchanged, current), None)

    result, _ = lax.scan(one_step, running, jnp.arange(count // block_rows, dtype=jnp.int32))
    return result


def body(queries, keys, values, doc_pos, log_decay, student_c, student_write, student_input, gain):
    tok_rows, head_count, head_width = queries.shape
    group_count = keys.shape[1]
    repeat = head_count // group_count
    state_width = student_c.shape[2]
    ctx_count = lax.axis_size("ctx")
    first_row = lax.axis_index("ctx") * tok_rows
    positions = first_row + jnp.arange(tok_rows, dtype=jnp.int32)
    doc_start = positions - doc_pos
    start_state = (
        jnp.full((head_count, tok_rows), NEG_FLOOR, jnp.float32),
        jnp.zeros((head_count, tok_rows, head_width), jnp.float32),
    )
    best, accum = fold_keys(
        start_state,
        (
            lax.all_gather(keys, "ctx", axis=0, tiled=True),
            lax.all_gather(values, "ctx", axis=0, tiled=True),
        ),
        queries,
        positions,
        doc_start,
    )
    teacher = accum / jnp.sqrt(jnp.mean(accum * accum, axis=-1, keepdims=True) + EPSILON)
    target = teacher.astype(jnp.bfloat16).transpose(1, 0, 2)
    log_level = jnp.cumsum(log_decay, axis=0)
    level_rows = log_level.T
    same_doc = (positions[None, :] <= positions[:, None]) & (
        positions[None, :] >= doc_start[:, None]
    )
    fade = jnp.exp(
        jnp.where(same_doc[None], level_rows[:, :, None] - level_rows[:, None, :], -jnp.inf)
    )
    grouped_readout = student_c.reshape(tok_rows, group_count, repeat, state_width)
    inner_product = jnp.einsum(
        "oizy,eiy->izoe", grouped_readout, student_write, preferred_element_type=jnp.float32
    )
    decay_kernel = (fade * inner_product.reshape(head_count, tok_rows, tok_rows)).astype(
        jnp.bfloat16
    )
    grouped_matrix = decay_kernel.reshape(group_count, repeat, tok_rows, tok_rows)
    within_block = jnp.einsum(
        "dlmx,xdc->mdlc", grouped_matrix, student_input, preferred_element_type=jnp.float32
    )
    within_block = within_block.reshape(tok_rows, head_count, head_width)
    last_start = doc_start[-1]
    tail_fade = jnp.where(
        (positions >= last_start)[:, None], jnp.exp(log_level[-1:, :] - log_level), 0.0
    )
    scaled_b = (
        tail_fade.reshape(tok_rows, group_count, repeat)[..., None] * student_write[:, :, None, :]
    ).astype(jnp.bfloat16)
    block_state = jnp.einsum(
        "tgrn,tgp->grnp", scaled_b, student_input, preferred_element_type=jnp.float32
    )
    block_state = block_state.reshape(head_count, state_width, head_width)
    block_decay = jnp.where(last_start < first_row, jnp.exp(log_level[-1]), 0.0)
    identity = (
        jnp.ones((head_count,), jnp.float32),
        jnp.zeros((head_count, state_width, head_width), jnp.float32),
    )
    _, carry_in = entering((block_decay, block_state), "ctx", chain_states, identity, False)
    head_fade = jnp.where((doc_start < first_row)[:, None], jnp.exp(log_level), 0.0)
    carry_low = carry_in.astype(jnp.bfloat16)
    from_carry = (
        jnp.einsum("thn,hnp->thp", student_c, carry_low, preferred_element_type=jnp.float32)
        * head_fade[..., None]
    )
    mixer = within_block + from_carry
    root_mean = jnp.sqrt(jnp.mean(mixer * mixer, axis=-1, keepdims=True) + STUDENT_FLOOR)
    normed = mixer / root_mean
    residual_diff = normed * gain[None] - target.astype(jnp.float32)
    gain_term = jnp.sum(residual_diff * normed, axis=0) / (tok_rows * ctx_count)
    grad_gain = lax.psum(gain_term, "ctx")
    scaled_diff = residual_diff * gain[None]
    mixer_grad = (
        (scaled_diff - normed * jnp.mean(scaled_diff * normed, axis=-1, keepdims=True)) / root_mean
    ).astype(jnp.bfloat16)
    faded_c = (head_fade[..., None] * student_c).astype(jnp.bfloat16)
    back_state = jnp.einsum("thn,thp->hnp", faded_c, mixer_grad, preferred_element_type=jnp.float32)
    _, carry_back = entering((block_decay, back_state), "ctx", chain_states, identity, True)
    back_low = carry_back.astype(jnp.bfloat16)
    grouped_gradient = mixer_grad.reshape(tok_rows, group_count, repeat, head_width)
    gradient_product = jnp.einsum(
        "zmhx,jmx->mhzj", grouped_gradient, student_input, preferred_element_type=jnp.float32
    )
    kernel_gradient = (fade * gradient_product.reshape(head_count, tok_rows, tok_rows)).astype(
        jnp.bfloat16
    )
    kernel_gradient = kernel_gradient.reshape(group_count, repeat, tok_rows, tok_rows)
    readout_gradient = jnp.einsum(
        "cmdu,ucx->dcmx", kernel_gradient, student_write, preferred_element_type=jnp.float32
    )
    readout_gradient = readout_gradient.reshape(tok_rows, head_count, state_width)
    readout_gradient = readout_gradient + head_fade[..., None] * jnp.einsum(
        "thp,hnp->thn", mixer_grad, carry_low, preferred_element_type=jnp.float32
    )
    grouped_fade = tail_fade.reshape(tok_rows, group_count, repeat, 1)
    grouped_back = back_low.reshape(group_count, repeat, state_width, head_width)
    write_gradient = jnp.einsum(
        "uyzx,zuye->xue", kernel_gradient, grouped_readout, preferred_element_type=jnp.float32
    )
    write_gradient = write_gradient + jnp.sum(
        grouped_fade
        * jnp.einsum(
            "grnp,sgp->sgrn", grouped_back, student_input, preferred_element_type=jnp.float32
        ),
        axis=2,
    )
    input_gradient = jnp.einsum(
        "uomb,muoz->buz", grouped_matrix, grouped_gradient, preferred_element_type=jnp.float32
    )
    input_gradient = input_gradient + jnp.sum(
        grouped_fade
        * jnp.einsum(
            "sgn,grnp->sgrp", student_write, grouped_back, preferred_element_type=jnp.float32
        ),
        axis=2,
    )
    return (
        readout_gradient.astype(jnp.bfloat16),
        write_gradient.astype(jnp.bfloat16),
        input_gradient.astype(jnp.bfloat16),
        grad_gain,
    )


def solution(mesh):
    placed = (
        P(("groups", "ctx"), "tp", None),
        P(("groups", "ctx"), "tp", None),
        P(("groups", "ctx"), "tp", None),
        P(("groups", "ctx")),
        P(("groups", "ctx"), "tp"),
        P(("groups", "ctx"), "tp", None),
        P(("groups", "ctx"), "tp", None),
        P(("groups", "ctx"), "tp", None),
        P("tp", None),
    )
    return jax.shard_map(
        body,
        mesh=mesh,
        in_specs=placed,
        out_specs=(
            P(("groups", "ctx"), "tp", None),
            P(("groups", "ctx"), "tp", None),
            P(("groups", "ctx"), "tp", None),
            P(("groups", "tp"), None),
        ),
        check_vma=False,
    )
```

profile of v0, /device:TPU:0, one launch (start us, length us, event | category | flops | bytes accessed | tf_op | source)
XLA Modules:
  0.0 225.4 jit_solution(7501806901297974506)
XLA Ops:
  12.1 2.4 %fusion.27 = f32[2,8,128,128]{3,2,1,0:T(8,128)} fusion(f32[256,2,128]{0,2,1:T(8,128)S(1)} %copy.120, f32[256,2,8]{0,2,1:T(8,128)S(1)} %get-tuple-element.705, bf16[256,2,128,1]{2,1,0,3:T(2,128)(2,1)} %bitcast.176), kind=kOutput, calls=%fused_computation.58 | convolution fusion | flops 135266304 | bytes 1458176 | tf_op jit(solution)/shard_map/tgrn,tgp->grnp/dot_general | solution.py:146
  14.8 1.6 copy.136
  18.9 24.2 %all_gather.23 = bf16[1024,2,128]{2,0,1:T(8,128)(2,1)} all-gather(bf16[256,2,128]{2,0,1:T(8,128)(2,1)S(1)} %copy.124), channel_id=1, replica_groups=mesh['groups'=2,'ctx'=4,'tp'=4] {'ctx'}, dimensions={0}, use_global_device_ids=true | all-gather | bytes 655360 | tf_op jit(solution)/shard_map/all_gather | solution.py:110
  43.2 21.8 %all_gather.24 = bf16[1024,2,128]{2,0,1:T(8,128)(2,1)} all-gather(bf16[256,2,128]{2,0,1:T(8,128)(2,1)S(1)} %copy.125), channel_id=1, replica_groups=mesh['groups'=2,'ctx'=4,'tp'=4] {'ctx'}, dimensions={0}, use_global_device_ids=true | all-gather | bytes 655360 | tf_op jit(solution)/shard_map/all_gather | solution.py:111
  65.2 11.3 %while.45 = (s32[]{:T(128)}, f32[16,256]{1,0:T(8,128)S(1)}, f32[16,256,128]{2,1,0:T(8,128)S(1)}, s32[2]{0:T(128)S(1)}, s32[]{:T(128)}, /*index=5*/s32[]{:T(128)}...) while((s32[]{:T(128)}, f32[16,256]{1,0:T(8,128)S(1)}, ...), condition=%wide.region_10.11_spmd.clone, body=%wide.region_6.10_spmd.clone.sunk | while | flops 1089868544 | bytes 29353344 | solution.py:90
  67.6 6.5 %conditional.3 = ((f32[16,256]{1,0:T(8,128)S(1)}, f32[16,256,128]{2,1,0:T(8,128)S(1)})) conditional(s32[]{:T(128)} %convert_element_type.113, (f32[16,256]{1,0:T(8,128)S(1)}, f32[16,256,128]{2,1,0:T(8,128)S(1)}) %tuple.134, (s32[]{:T(128)}, s32[]{:T(128)}, s32[256]{0:T(256)S(1)}, bf16[1024,2,128]{2,0,1:T(8,128)(2,1)}, ...), branch_computations={%region_7.7_spmd, %region_8.9_spmd} | conditional | flops 1089868544 | bytes 29352038 | solution.py:88
  67.8 2.7 %fusion.2 = (f32[2,8,256]{2,1,0:T(8,128)S(1)}, f32[2,512,256,8]{2,1,3,0:T(8,128)S(1)}) fusion(pred[256,512]{0,1:T(8,128)(4,1)S(1)} %compare_and_fusion, bf16[256,2,8,128]{3,0,2,1:T(8,128)(2,1)} %bitcast.163, bf16[1024,2,128]{2,0,1:T(8,128)(2,1)} %get-tuple-element.492, s32[]{:T(128)S(6)} %select_n.74), kind=kOutput, calls=%fused_computation.3 | convolution fusion | flops 543158272 | bytes 9846788 | tf_op jit(solution)/shard_map/while/body/eval_jaxpr/cond/branch_1_fun/yubk,ouk->ubyo/dot_general | solution.py:46
  70.5 2.5 %fusion.3 = f32[2,8,256,128]{3,2,1,0:T(8,128)S(1)} fusion(f32[2,512,256,8]{2,1,3,0:T(8,128)S(1)} %get-tuple-element.704, f32[2,8,256]{2,1,0:T(8,128)S(1)} %bitcast.170, pred[256,512]{0,1:T(8,128)(4,1)S(1)} %compare_and_fusion, bf16[1024,2,128]{2,0,1:T(8,128)(2,1)S(1)} %copy-done.12, s32[]{:T(128)S(6)} %select_n.74), kind=kOutput, calls=%fused_computation.4 | convolution fusion | flops 545259520 | bytes 10895364 | tf_op jit(solution)/shard_map/while/body/eval_jaxpr/cond/branch_1_fun/hvbc,chw->hvbw/dot_general | solution.py:55
  76.5 1.9 copy.127
  78.3 18.3 %all-gather.1 = f32[4,1,16]{2,1,0:T(1,128)S(1)} all-gather(f32[1,1,16]{2,1,0:T(1,128)S(1)} %bitcast.181), channel_id=1, replica_groups=mesh['groups'=2,'ctx'=4,'tp'=4] {'ctx'}, dimensions={0}, use_global_device_ids=true | all-gather | bytes 320 | tf_op jit(solution)/shard_map/all_gather | solution.py:14
  100.2 1.8 fusion.39
  102.1 9.2 %all-gather.5.cloned.1.call-done = f32[4,16,128,128]{3,2,1,0:T(8,128)} async-done(((f32[1,16,128,128]{3,2,1,0:T(8,128)}), f32[4,16,128,128]{3,2,1,0:T(8,128)}) %all-gather.5.cloned.1.call-update) | async-done | bytes 4194320 | tf_op jit(solution)/shard_map/all_gather | solution.py:14
  111.3 4.5 %while.46 = (s32[]{:T(128)}, f32[16,128,128]{2,1,0:T(8,128)S(1)}, s32[]{:T(128)}, f32[4,16]{1,0:T(4,128)S(1)}, f32[4,16,128,128]{3,2,1,0:T(8,128)}, /*index=5*/s32[]{:T(128)}, s32[]{:T(128)}) while((s32[]{:T(128)}, f32[16,128,128]{2,1,0:T(8,128)S(1)}, s32[]{:T(128)}, f32[4,16]{1,0:T(4,128)S(1)}, f32[4,16,128,128]{3,2,1,0:T(8,128)}, ...), condition=%wide.region_3.4_spmd.clone, body=%wide.region_2.0_spmd.clone.sunk | while | flops 1048580 | bytes 3146025 | solution.py:26
  111.3 1.5 fusion.65
  115.8 2.3 %multiply_reduce_fusion.3 = (f32[256,16]{0,1:T(8,128)S(1)}, f32[256,16,128]{0,2,1:T(8,128)S(1)}) fusion(f32[256,16]{0,1:T(8,128)S(1)} %get-tuple-element.706, bf16[256,16,128]{0,2,1:T(8,128)(2,1)S(1)} %copy-done.1, f32[16,128,128]{2,1,0:T(8,128)S(1)} %get-tuple-element.523, f32[2,8,256,128]{2,3,1,0:T(8,128)} %fusion.39), kind=kOutput, calls=%fused_computation.49 | convolution fusion | flops 136572928 | bytes 6324224 | tf_op jit(solution)/shard_map/thn,hnp->thp/dot_general | solution.py:159
  124.3 2.3 %convolution_bitcast_fusion = f32[256,2,8,128]{3,0,2,1:T(8,128)} fusion(bf16[2,8,256,256]{2,3,1,0:T(8,128)(2,1)S(1)} %fusion.16, bf16[256,2,128,1]{2,1,0,3:T(2,128)(2,1)S(1)} %bitcast.174), kind=kOutput, calls=%fused_computation.51 | convolution fusion | flops 268435456 | bytes 4325376 | tf_op jit(solution)/shard_map/cmdu,ucx->dcmx/dot_general | solution.py:184
  126.6 3.0 %copy.133 = f32[256,2,8,128]{0,3,2,1:T(8,128)} copy(f32[256,2,8,128]{3,0,2,1:T(8,128)} %convolution_bitcast_fusion) | data formatting | bytes 4194304 | tf_op jit(solution)/shard_map/cmdu,ucx->dcmx/transpose | solution.py:184
  129.5 3.1 %fusion.21 = bf16[256,16,128]{0,2,1:T(8,128)(2,1)} fusion(f32[256,2,8,128]{0,3,2,1:T(8,128)} %copy.133, bf16[256,16,128]{0,2,1:T(8,128)(2,1)S(1)} %divide_convert_fusion, f32[256,16]{0,1:T(8,128)S(1)} %get-tuple-element.706, f32[16,128,128]{2,1,0:T(8,128)S(1)} %get-tuple-element.523), kind=kOutput, calls=%fused_computation.39 | convolution fusion | flops 136052736 | bytes 5259264 | tf_op jit(solution)/shard_map/thp,hnp->thn/dot_general | solution.py:188
  132.7 2.6 %copy.143 = bf16[256,16,128]{2,1,0:T(8,128)(2,1)} copy(bf16[256,16,128]{0,2,1:T(8,128)(2,1)} %fusion.21) | data formatting | bytes 2097152
  135.3 11.9 %psum.7 = f32[16,128]{1,0:T(8,128)} all-reduce(f32[16,128]{1,0:T(8,128)S(1)} %broadcast_multiply_fusion.1), channel_id=1, replica_groups=mesh['groups'=2,'ctx'=4,'tp'=4] {'ctx'}, use_global_device_ids=true, to_apply=%region_18.19 | all-reduce | flops 2048 | bytes 16384 | tf_op jit(solution)/shard_map/psum | solution.py:167
  147.2 55.8 %all-gather.7.cloned.1.call-done = f32[64,128,128]{2,1,0:T(8,128)} async-done(((f32[16,128,128]{2,1,0:T(8,128)}), f32[64,128,128]{2,1,0:T(8,128)}) %all-gather.7.cloned.1.call-update) | async-done | bytes 4194320 | tf_op jit(solution)/shard_map/all_gather | solution.py:14
  203.0 4.7 %rev.7 = f32[4,16,128,128]{3,2,1,0:T(8,128)} reverse(f32[4,16,128,128]{3,2,1,0:T(8,128)} %bitcast.168), dimensions={0} | reverse | bytes 8388608 | tf_op jit(solution)/shard_map/rev | solution.py:16
  207.6 4.5 %while.47 = (s32[]{:T(128)}, f32[16,128,128]{2,1,0:T(8,128)S(1)}, s32[]{:T(128)}, f32[4,16]{1,0:T(4,128)S(1)}, f32[4,16,128,128]{3,2,1,0:T(8,128)}, /*index=5*/s32[]{:T(128)}, s32[]{:T(128)}) while((s32[]{:T(128)}, f32[16,128,128]{2,1,0:T(8,128)S(1)}, s32[]{:T(128)}, f32[4,16]{1,0:T(4,128)S(1)}, f32[4,16,128,128]{3,2,1,0:T(8,128)}, ...), condition=%wide.region_14.15_spmd.clone, body=%wide.region_13.14_spmd.clone.sunk | while | flops 1048580 | bytes 3146025 | solution.py:26
  215.4 2.3 %fusion.26 = bf16[256,2,128]{2,0,1:T(8,128)(2,1)S(1)} fusion(f32[256,2,128]{2,0,1:T(8,128)S(1)} %copy.139, bf16[2,8,256,256]{2,3,1,0:T(8,128)(2,1)} %copy-done.4, bf16[256,2,8,128]{3,2,1,0:T(8,128)(2,1)S(1)} %bitcast.167), kind=kOutput, calls=%fused_computation.57 | convolution fusion | flops 268566528 | bytes 3538944 | tf_op jit(solution)/shard_map/uyzx,zuye->xue/dot_general | solution.py:193
  (102 shorter events, 30.5 us)
Async XLA Ops:
  7.2 2.7 %copy-start = (f32[256,16]{0,1:T(8,128)S(1)}, f32[256,16]{0,1:T(8,128)}, u32[]{:S(2)}) copy-start(f32[256,16]{0,1:T(8,128)} %param.21) | copy-start | bytes 49156
  7.2 7.6 %copy-start.6 = (bf16[256,16,128]{2,1,0:T(8,128)(2,1)S(1)}, bf16[256,16,128]{2,1,0:T(8,128)(2,1)}, u32[]{:S(2)}) copy-start(bf16[256,16,128]{2,1,0:T(8,128)(2,1)} %param.22) | copy-start | bytes 3145732
  7.2 104.1 %all-gather.5.cloned.1.call-start = ((), (), s32[]{:S(2)}) async-start(), calls=%async_computation | async-start | bytes 5242880 | tf_op jit(solution)/shard_map/all_gather | solution.py:14
  12.1 5.5 %copy-start.9 = (bf16[256,16,128]{2,1,0:T(8,128)(2,1)S(1)}, bf16[256,16,128]{2,1,0:T(8,128)(2,1)}, u32[]{:S(2)}) copy-start(bf16[256,16,128]{2,1,0:T(8,128)(2,1)} %param.17) | copy-start | bytes 3145732
  14.6 188.4 %all-gather.7.cloned.1.call-start = ((), (), s32[]{:S(2)}) async-start(), calls=%async_computation.1 | async-start | bytes 5242880 | tf_op jit(solution)/shard_map/all_gather | solution.py:14
  14.8 4.1 %copy-start.13 = (bf16[256,2,128]{2,1,0:T(2,128)(2,1)S(1)}, bf16[256,2,128]{2,1,0:T(2,128)(2,1)}, u32[]{:S(2)}) copy-start(bf16[256,2,128]{2,1,0:T(2,128)(2,1)} %param.18) | copy-start | bytes 393220
  14.8 4.1 %copy-start.14 = (bf16[256,2,128]{2,1,0:T(2,128)(2,1)S(1)}, bf16[256,2,128]{2,1,0:T(2,128)(2,1)}, u32[]{:S(2)}) copy-start(bf16[256,2,128]{2,1,0:T(2,128)(2,1)} %param.19) | copy-start | bytes 393220
  67.8 2.8 %copy-start.12 = (bf16[1024,2,128]{2,0,1:T(8,128)(2,1)S(1)}, bf16[1024,2,128]{2,0,1:T(8,128)(2,1)}, u32[]{:S(2)}) copy-start(bf16[1024,2,128]{2,0,1:T(8,128)(2,1)} %get-tuple-element.495) | copy-start | bytes 1572868 | tf_op jit(solution)/shard_map/while/body/eval_jaxpr/cond
  78.3 19.1 %copy-start.7 = (bf16[256,16,128]{2,1,0:T(8,128)(2,1)S(1)}, bf16[256,16,128]{2,1,0:T(8,128)(2,1)}, u32[]{:S(2)}) copy-start(bf16[256,16,128]{2,1,0:T(8,128)(2,1)} %param.22) | copy-start | bytes 3145732
  78.3 19.1 %copy-start.10 = (bf16[256,2,128]{2,1,0:T(2,128)(2,1)S(1)}, bf16[256,2,128]{2,1,0:T(2,128)(2,1)}, u32[]{:S(2)}) copy-start(bf16[256,2,128]{2,1,0:T(2,128)(2,1)} %param.23) | copy-start | bytes 393220
  97.4 2.8 %copy-start.11 = (bf16[256,2,128]{2,1,0:T(2,128)(2,1)S(1)}, bf16[256,2,128]{2,1,0:T(2,128)(2,1)}, u32[]{:S(2)}) copy-start(bf16[256,2,128]{2,1,0:T(2,128)(2,1)} %param.24) | copy-start | bytes 393220
  98.8 1.4 copy-start.2
  111.3 4.6 %copy-start.1 = (bf16[256,16,128]{0,2,1:T(8,128)(2,1)S(1)}, bf16[256,16,128]{0,2,1:T(8,128)(2,1)}, u32[]{:S(2)}) copy-start(bf16[256,16,128]{0,2,1:T(8,128)(2,1)} %copy.136) | copy-start | bytes 3145732
  115.8 2.4 %copy-start.5 = (f32[16,256,128]{1,2,0:T(8,128)S(1)}, f32[16,256,128]{1,2,0:T(8,128)}, u32[]{:S(2)}) copy-start(f32[16,256,128]{1,2,0:T(8,128)} %copy.127) | copy-start | bytes 6291460
  115.8 2.4 %copy-start.15 = (f32[16,128]{1,0:T(8,128)S(1)}, f32[16,128]{1,0:T(8,128)}, u32[]{:S(2)}) copy-start(f32[16,128]{1,0:T(8,128)} %param.25) | copy-start | bytes 24580
  123.0 1.3 copy-start.4
  212.1 1.6 copy-start.3
  213.7 1.7 copy-start.8
Sparse Core Ops, SparseCore 0:
  14.7 96.5 all-gather.4
  121.8 81.0 all-gather.6
where the time goes:
time: 226 us; the launch traced here: 225 us
  blocking collectives  76.2 us (34%)
  waiting for transfers between devices  65 us (29%)
  matrix products  25.4 us (11%)
  local copies, waits for them, and re-layouts  23.8 us (11%)
  other arithmetic  15.9 us (7%)
  between operations  15.1 us (7%)
  loops' own time  3.88 us (2%)
    all_gather x2, waiting for transfers between devices, entering(): pieces = jax.tree.map(lambda part: lax.all_gather(part, axis), value)  65 us
    all_gather x1, blocking collectives, body(): lax.all_gather(keys, 'ctx', axis=0, tiled=True)  24.2 us
    all_gather x1, blocking collectives, body(): lax.all_gather(values, 'ctx', axis=0, tiled=True)  21.8 us
    all_gather x1, blocking collectives, entering(): pieces = jax.tree.map(lambda part: lax.all_gather(part, axis), value)  18.3 us
    psum x1, blocking collectives, body(): grad_gain = lax.psum(gain_term, 'ctx')  11.9 us
    unnamed x37, local copies, waits for them, and re-layouts  10.3 us
    select_n x6, other arithmetic, step(): jnp.where(position < mine, new, old)  8.83 us
    rev x2, local copies, waits for them, and re-layouts, entering(): pieces = jax.tree.map(lambda part: part[::-1], pieces)  4.68 us
  transfers between devices with their start and end apart: 2, of which 2 were waited for; matrix products, arithmetic and copies ran while one was open for 13% of the time, Pallas kernels for 0%

commit v1 on v0

--- a/solution.py
+++ b/solution.py
@@ -164,7 +164,11 @@
     normed = mixer / root_mean
     residual_diff = normed * gain[None] - target.astype(jnp.float32)
     gain_term = jnp.sum(residual_diff * normed, axis=0) / (tok_rows * ctx_count)
-    grad_gain = lax.psum(gain_term, "ctx")
+    grad_gain = gain_term
+    for hop in (1, 2):
+        grad_gain = grad_gain + lax.ppermute(
+            grad_gain, "ctx", [(dev, dev ^ hop) for dev in range(4)]
+        )
     scaled_diff = residual_diff * gain[None]
     mixer_grad = (
         (scaled_diff - normed * jnp.mean(scaled_diff * normed, axis=-1, keepdims=True)) / root_mean

time: 226 us -> 228 us (level)
  blocking collectives: 76.2 us -> 64.3 us
  waiting for transfers between devices: 65 us -> 72.2 us
  local copies, waits for them, and re-layouts: 23.8 us -> 26.6 us
  starting transfers between devices: 0.08 us -> 2.76 us
    psum x1 -> x0, blocking collectives: 11.9 us -> none  [body(): grad_gain = lax.psum(gain_term, 'ctx')]
    all_gather x2, waiting for transfers between devices: 65 us -> 72.1 us  [entering(): pieces = jax.tree.map(lambda part: lax.all_gather(part, axis), value)]
    ppermute x0 -> x2, starting transfers between devices: none -> 2.68 us  [body(): lax.ppermute(grad_gain, 'ctx', [(dev, dev ^ hop) for dev in range(4)])]
  transfers between devices with their start and end apart: 2 -> 4, of which waited for: 2 -> 2; matrix products, arithmetic and copies ran while one was open for 13% -> 14% of each run, Pallas kernels for 0% -> 0%
where the time goes in v1:
time: 228 us; the launch traced here: 227 us
  waiting for transfers between devices  72.2 us (32%)
  blocking collectives  64.3 us (28%)
  local copies, waits for them, and re-layouts  26.6 us (12%)
  matrix products  25.3 us (11%)
  other arithmetic  17.1 us (8%)
  between operations  15.1 us (7%)
  loops' own time  3.85 us (2%)
  starting transfers between devices  2.76 us (1%)
    all_gather x2, waiting for transfers between devices, entering(): pieces = jax.tree.map(lambda part: lax.all_gather(part, axis), value)  72.1 us
    all_gather x1, blocking collectives, body(): lax.all_gather(keys, 'ctx', axis=0, tiled=True)  24.2 us
    all_gather x1, blocking collectives, body(): lax.all_gather(values, 'ctx', axis=0, tiled=True)  21.8 us
    all_gather x1, blocking collectives, entering(): pieces = jax.tree.map(lambda part: lax.all_gather(part, axis), value)  18.3 us
    unnamed x37, local copies, waits for them, and re-layouts  10.4 us
    select_n x6, other arithmetic, step(): jnp.where(position < mine, new, old)  8.82 us
    rev x2, local copies, waits for them, and re-layouts, entering(): pieces = jax.tree.map(lambda part: part[::-1], pieces)  5.25 us
  transfers between devices with their start and end apart: 4, of which 2 were waited for; matrix products, arithmetic and copies ran while one was open for 14% of the time, Pallas kernels for 0%

profile of v1, /device:TPU:0, one launch (start us, length us, event | category | flops | bytes accessed | tf_op | source)
XLA Modules:
  0.0 227.2 jit_solution(12257455862373021125)
XLA Ops:
  12.1 2.4 %fusion.27 = f32[2,8,128,128]{3,2,1,0:T(8,128)} fusion(f32[256,2,128]{0,2,1:T(8,128)S(1)} %copy.120, f32[256,2,8]{0,2,1:T(8,128)S(1)} %get-tuple-element.705, bf16[256,2,128,1]{2,1,0,3:T(2,128)(2,1)} %bitcast.176), kind=kOutput, calls=%fused_computation.58 | convolution fusion | flops 135266304 | bytes 1458176 | tf_op jit(solution)/shard_map/tgrn,tgp->grnp/dot_general | solution.py:146
  14.8 1.6 copy.136
  18.9 24.2 %all_gather.23 = bf16[1024,2,128]{2,0,1:T(8,128)(2,1)} all-gather(bf16[256,2,128]{2,0,1:T(8,128)(2,1)S(1)} %copy.124), channel_id=1, replica_groups=mesh['groups'=2,'ctx'=4,'tp'=4] {'ctx'}, dimensions={0}, use_global_device_ids=true | all-gather | bytes 655360 | tf_op jit(solution)/shard_map/all_gather | solution.py:110
  43.2 21.8 %all_gather.24 = bf16[1024,2,128]{2,0,1:T(8,128)(2,1)} all-gather(bf16[256,2,128]{2,0,1:T(8,128)(2,1)S(1)} %copy.125), channel_id=1, replica_groups=mesh['groups'=2,'ctx'=4,'tp'=4] {'ctx'}, dimensions={0}, use_global_device_ids=true | all-gather | bytes 655360 | tf_op jit(solution)/shard_map/all_gather | solution.py:111
  65.2 11.3 %while.45 = (s32[]{:T(128)}, f32[16,256]{1,0:T(8,128)S(1)}, f32[16,256,128]{2,1,0:T(8,128)S(1)}, s32[2]{0:T(128)S(1)}, s32[]{:T(128)}, /*index=5*/s32[]{:T(128)}...) while((s32[]{:T(128)}, f32[16,256]{1,0:T(8,128)S(1)}, ...), condition=%wide.region_10.11_spmd.clone, body=%wide.region_6.10_spmd.clone.sunk | while | flops 1089868544 | bytes 29353344 | solution.py:90
  67.5 6.5 %conditional.3 = ((f32[16,256]{1,0:T(8,128)S(1)}, f32[16,256,128]{2,1,0:T(8,128)S(1)})) conditional(s32[]{:T(128)} %convert_element_type.113, (f32[16,256]{1,0:T(8,128)S(1)}, f32[16,256,128]{2,1,0:T(8,128)S(1)}) %tuple.134, (s32[]{:T(128)}, s32[]{:T(128)}, s32[256]{0:T(256)S(1)}, bf16[1024,2,128]{2,0,1:T(8,128)(2,1)}, ...), branch_computations={%region_7.7_spmd, %region_8.9_spmd} | conditional | flops 1089868544 | bytes 29352038 | solution.py:88
  67.8 2.7 %fusion.2 = (f32[2,8,256]{2,1,0:T(8,128)S(1)}, f32[2,512,256,8]{2,1,3,0:T(8,128)S(1)}) fusion(pred[256,512]{0,1:T(8,128)(4,1)S(1)} %compare_and_fusion, bf16[256,2,8,128]{3,0,2,1:T(8,128)(2,1)} %bitcast.163, bf16[1024,2,128]{2,0,1:T(8,128)(2,1)} %get-tuple-element.492, s32[]{:T(128)S(6)} %select_n.74), kind=kOutput, calls=%fused_computation.3 | convolution fusion | flops 543158272 | bytes 9846788 | tf_op jit(solution)/shard_map/while/body/eval_jaxpr/cond/branch_1_fun/yubk,ouk->ubyo/dot_general | solution.py:46
  70.5 2.5 %fusion.3 = f32[2,8,256,128]{3,2,1,0:T(8,128)S(1)} fusion(f32[2,512,256,8]{2,1,3,0:T(8,128)S(1)} %get-tuple-element.704, f32[2,8,256]{2,1,0:T(8,128)S(1)} %bitcast.170, pred[256,512]{0,1:T(8,128)(4,1)S(1)} %compare_and_fusion, bf16[1024,2,128]{2,0,1:T(8,128)(2,1)S(1)} %copy-done.12, s32[]{:T(128)S(6)} %select_n.74), kind=kOutput, calls=%fused_computation.4 | convolution fusion | flops 545259520 | bytes 10895364 | tf_op jit(solution)/shard_map/while/body/eval_jaxpr/cond/branch_1_fun/hvbc,chw->hvbw/dot_general | solution.py:55
  76.4 1.9 copy.127
  78.3 18.3 %all-gather.1 = f32[4,1,16]{2,1,0:T(1,128)S(1)} all-gather(f32[1,1,16]{2,1,0:T(1,128)S(1)} %bitcast.181), channel_id=1, replica_groups=mesh['groups'=2,'ctx'=4,'tp'=4] {'ctx'}, dimensions={0}, use_global_device_ids=true | all-gather | bytes 320 | tf_op jit(solution)/shard_map/all_gather | solution.py:14
  100.2 1.8 fusion.39
  102.1 9.2 %all-gather.5.cloned.1.call-done = f32[4,16,128,128]{3,2,1,0:T(8,128)} async-done(((f32[1,16,128,128]{3,2,1,0:T(8,128)}), f32[4,16,128,128]{3,2,1,0:T(8,128)}) %all-gather.5.cloned.1.call-update) | async-done | bytes 4194320 | tf_op jit(solution)/shard_map/all_gather | solution.py:14
  111.3 4.5 %while.46 = (s32[]{:T(128)}, f32[16,128,128]{2,1,0:T(8,128)S(1)}, s32[]{:T(128)}, f32[4,16]{1,0:T(4,128)S(1)}, f32[4,16,128,128]{3,2,1,0:T(8,128)}, /*index=5*/s32[]{:T(128)}, s32[]{:T(128)}) while((s32[]{:T(128)}, f32[16,128,128]{2,1,0:T(8,128)S(1)}, s32[]{:T(128)}, f32[4,16]{1,0:T(4,128)S(1)}, f32[4,16,128,128]{3,2,1,0:T(8,128)}, ...), condition=%wide.region_3.4_spmd.clone, body=%wide.region_2.0_spmd.clone.sunk | while | flops 1048580 | bytes 3146025 | solution.py:26
  111.3 1.5 fusion.66
  115.8 2.3 %multiply_reduce_fusion.3 = (f32[256,16]{0,1:T(8,128)S(1)}, f32[256,16,128]{0,2,1:T(8,128)S(1)}) fusion(f32[256,16]{0,1:T(8,128)S(1)} %get-tuple-element.706, bf16[256,16,128]{0,2,1:T(8,128)(2,1)S(1)} %copy-done.1, f32[16,128,128]{2,1,0:T(8,128)S(1)} %get-tuple-element.523, f32[2,8,256,128]{2,3,1,0:T(8,128)} %fusion.39), kind=kOutput, calls=%fused_computation.49 | convolution fusion | flops 136572928 | bytes 6324224 | tf_op jit(solution)/shard_map/thn,hnp->thp/dot_general | solution.py:159
  126.2 2.3 %convolution_bitcast_fusion = f32[256,2,8,128]{3,0,2,1:T(8,128)} fusion(bf16[2,8,256,256]{2,3,1,0:T(8,128)(2,1)S(1)} %fusion.16, bf16[256,2,128,1]{2,1,0,3:T(2,128)(2,1)S(1)} %bitcast.174), kind=kOutput, calls=%fused_computation.51 | convolution fusion | flops 268435456 | bytes 4325376 | tf_op jit(solution)/shard_map/cmdu,ucx->dcmx/dot_general | solution.py:188
  128.5 3.1 %copy.133 = f32[256,2,8,128]{0,3,2,1:T(8,128)} copy(f32[256,2,8,128]{3,0,2,1:T(8,128)} %convolution_bitcast_fusion) | data formatting | bytes 4194304 | tf_op jit(solution)/shard_map/cmdu,ucx->dcmx/transpose | solution.py:188
  131.7 1.9 collective-permute-start.1
  133.6 3.0 %fusion.21 = bf16[256,16,128]{0,2,1:T(8,128)(2,1)} fusion(f32[256,2,8,128]{0,3,2,1:T(8,128)} %copy.133, bf16[256,16,128]{0,2,1:T(8,128)(2,1)S(1)} %divide_convert_fusion, f32[256,16]{0,1:T(8,128)S(1)} %get-tuple-element.706, f32[16,128,128]{2,1,0:T(8,128)S(1)} %get-tuple-element.523), kind=kOutput, calls=%fused_computation.39 | convolution fusion | flops 136052736 | bytes 5259264 | tf_op jit(solution)/shard_map/thp,hnp->thn/dot_general | solution.py:192
  136.6 2.6 %copy.143 = bf16[256,16,128]{2,1,0:T(8,128)(2,1)} copy(bf16[256,16,128]{0,2,1:T(8,128)(2,1)} %fusion.21) | data formatting | bytes 2097152
  139.8 62.9 %all-gather.7.cloned.1.call-done = f32[64,128,128]{2,1,0:T(8,128)} async-done(((f32[16,128,128]{2,1,0:T(8,128)}), f32[64,128,128]{2,1,0:T(8,128)}) %all-gather.7.cloned.1.call-update) | async-done | bytes 4194320 | tf_op jit(solution)/shard_map/all_gather | solution.py:14
  202.8 4.7 %rev.7 = f32[4,16,128,128]{3,2,1,0:T(8,128)} reverse(f32[4,16,128,128]{3,2,1,0:T(8,128)} %bitcast.168), dimensions={0} | reverse | bytes 8388608 | tf_op jit(solution)/shard_map/rev | solution.py:16
  207.4 6.5 %while.47 = (s32[]{:T(128)}, f32[16,128,128]{2,1,0:T(8,128)S(1)}, s32[]{:T(128)}, f32[4,16]{1,0:T(4,128)}, f32[4,16,128,128]{3,2,1,0:T(8,128)}, /*index=5*/s32[]{:T(128)}, s32[]{:T(128)}) while((s32[]{:T(128)}, f32[16,128,128]{2,1,0:T(8,128)S(1)}, s32[]{:T(128)}, f32[4,16]{1,0:T(4,128)}, f32[4,16,128,128]{3,2,1,0:T(8,128)}, ...), condition=%wide.region_14.15_spmd.clone, body=%wide.region_13.14_spmd.clone.sunk | while | flops 1048580 | bytes 3146025 | solution.py:26
  217.2 2.3 %fusion.26 = bf16[256,2,128]{2,0,1:T(8,128)(2,1)S(1)} fusion(f32[256,2,128]{2,0,1:T(8,128)S(1)} %copy.139, bf16[2,8,256,256]{2,3,1,0:T(8,128)(2,1)} %copy-done.4, bf16[256,2,8,128]{3,2,1,0:T(8,128)(2,1)S(1)} %bitcast.167), kind=kOutput, calls=%fused_computation.57 | convolution fusion | flops 268566528 | bytes 3538944 | tf_op jit(solution)/shard_map/uyzx,zuye->xue/dot_general | solution.py:197
  (107 shorter events, 35.1 us)
Async XLA Ops:
  7.2 2.7 %copy-start = (f32[256,16]{0,1:T(8,128)S(1)}, f32[256,16]{0,1:T(8,128)}, u32[]{:S(2)}) copy-start(f32[256,16]{0,1:T(8,128)} %param.21) | copy-start | bytes 49156
  7.2 7.6 %copy-start.6 = (bf16[256,16,128]{2,1,0:T(8,128)(2,1)S(1)}, bf16[256,16,128]{2,1,0:T(8,128)(2,1)}, u32[]{:S(2)}) copy-start(bf16[256,16,128]{2,1,0:T(8,128)(2,1)} %param.22) | copy-start | bytes 3145732
  7.2 104.1 %all-gather.5.cloned.1.call-start = ((), (), s32[]{:S(2)}) async-start(), calls=%async_computation | async-start | bytes 5242880 | tf_op jit(solution)/shard_map/all_gather | solution.py:14
  12.1 5.5 %copy-start.9 = (bf16[256,16,128]{2,1,0:T(8,128)(2,1)S(1)}, bf16[256,16,128]{2,1,0:T(8,128)(2,1)}, u32[]{:S(2)}) copy-start(bf16[256,16,128]{2,1,0:T(8,128)(2,1)} %param.17) | copy-start | bytes 3145732
  14.6 188.2 %all-gather.7.cloned.1.call-start = ((), (), s32[]{:S(2)}) async-start(), calls=%async_computation.1 | async-start | bytes 5242880 | tf_op jit(solution)/shard_map/all_gather | solution.py:14
  14.8 4.1 %copy-start.13 = (bf16[256,2,128]{2,1,0:T(2,128)(2,1)S(1)}, bf16[256,2,128]{2,1,0:T(2,128)(2,1)}, u32[]{:S(2)}) copy-start(bf16[256,2,128]{2,1,0:T(2,128)(2,1)} %param.18) | copy-start | bytes 393220
  14.8 4.1 %copy-start.14 = (bf16[256,2,128]{2,1,0:T(2,128)(2,1)S(1)}, bf16[256,2,128]{2,1,0:T(2,128)(2,1)}, u32[]{:S(2)}) copy-start(bf16[256,2,128]{2,1,0:T(2,128)(2,1)} %param.19) | copy-start | bytes 393220
  67.8 2.8 %copy-start.12 = (bf16[1024,2,128]{2,0,1:T(8,128)(2,1)S(1)}, bf16[1024,2,128]{2,0,1:T(8,128)(2,1)}, u32[]{:S(2)}) copy-start(bf16[1024,2,128]{2,0,1:T(8,128)(2,1)} %get-tuple-element.495) | copy-start | bytes 1572868 | tf_op jit(solution)/shard_map/while/body/eval_jaxpr/cond
  78.3 19.1 %copy-start.7 = (bf16[256,16,128]{2,1,0:T(8,128)(2,1)S(1)}, bf16[256,16,128]{2,1,0:T(8,128)(2,1)}, u32[]{:S(2)}) copy-start(bf16[256,16,128]{2,1,0:T(8,128)(2,1)} %param.22) | copy-start | bytes 3145732
  78.3 19.1 %copy-start.10 = (bf16[256,2,128]{2,1,0:T(2,128)(2,1)S(1)}, bf16[256,2,128]{2,1,0:T(2,128)(2,1)}, u32[]{:S(2)}) copy-start(bf16[256,2,128]{2,1,0:T(2,128)(2,1)} %param.23) | copy-start | bytes 393220
  97.4 2.8 %copy-start.11 = (bf16[256,2,128]{2,1,0:T(2,128)(2,1)S(1)}, bf16[256,2,128]{2,1,0:T(2,128)(2,1)}, u32[]{:S(2)}) copy-start(bf16[256,2,128]{2,1,0:T(2,128)(2,1)} %param.24) | copy-start | bytes 393220
  98.8 1.4 copy-start.2
  111.3 4.6 %copy-start.1 = (bf16[256,16,128]{0,2,1:T(8,128)(2,1)S(1)}, bf16[256,16,128]{0,2,1:T(8,128)(2,1)}, u32[]{:S(2)}) copy-start(bf16[256,16,128]{0,2,1:T(8,128)(2,1)} %copy.136) | copy-start | bytes 3145732
  115.8 2.4 %copy-start.5 = (f32[16,256,128]{1,2,0:T(8,128)S(1)}, f32[16,256,128]{1,2,0:T(8,128)}, u32[]{:S(2)}) copy-start(f32[16,256,128]{1,2,0:T(8,128)} %copy.127) | copy-start | bytes 6291460
  115.8 2.4 %copy-start.15 = (f32[16,128]{1,0:T(8,128)S(1)}, f32[16,128]{1,0:T(8,128)}, u32[]{:S(2)}) copy-start(f32[16,128]{1,0:T(8,128)} %param.25) | copy-start | bytes 24580
  122.9 8.8 %collective-permute-start = (f32[16,128]{1,0:T(8,128)}, f32[16,128]{1,0:T(8,128)S(1)}, u32[]{:S(2)}, u32[]{:S(2)}) collective-permute-start(f32[16,128]{1,0:T(8,128)} %broadcast_multiply_fusion.1), channel_id=1, source_target_pairs={{0,4},{4,0},{8,12},{12,8},{1,5},{5,1},{9,13},{13,9},{2,6},{6,2},{1... | collective-permute-start | bytes 24584 | tf_op jit(solution)/shard_map/ppermute | solution.py:169
  124.9 1.3 copy-start.4
  131.7 7.6 %collective-permute-start.1 = (f32[16,128]{1,0:T(8,128)S(1)}, f32[16,128]{1,0:T(8,128)S(1)}, u32[]{:S(2)}, u32[]{:S(2)}) collective-permute-start(f32[16,128]{1,0:T(8,128)S(1)} %fusion.46), channel_id=1, source_target_pairs={{0,8},{4,12},{8,0},{12,4},{1,9},{5,13},{9,1},{13,5},{2,10},{6,14},... | collective-permute-start | bytes 24584 | tf_op jit(solution)/shard_map/ppermute | solution.py:169
  213.9 1.6 copy-start.3
  215.5 1.7 copy-start.8
Sparse Core Ops, SparseCore 0:
  14.7 96.5 all-gather.4
  121.8 80.9 all-gather.6
